TPU v7x, 32 devices: a whole 2x2x4 slice. The times are simulated.
32 devices in a mesh: orb: 8 (over z, core), aux: 4 (over y, x).
Axes of the slice: x: 2, y: 2, z: 4, core: 2. Of those that a mesh axis runs over, the one named last changes fastest.
Arguments:
- three_centre: bfloat16 [32, 4096, 384], P('aux', 'orb'), may hold values from -6 to 6
- b_screen: int32 [32, 3], P('orb'), may hold values 0 or 1
- g_occ: bfloat16 [4096, 384], P('orb'), may hold values from -0.0068359375 to 0.0068359375
- occ_screen: int32 [32, 3], P('orb'), may hold values 0 or 1
- g_vir: bfloat16 [4096, 384], P('orb'), may hold values from -0.0068359375 to 0.0068359375
- vir_screen: int32 [32, 3], P('orb'), may hold values 0 or 1
Outputs:
- response: float32 [32, 32], P('aux')
All inputs are finite; a program needn't handle non-finite values. No bound on the sum of `b_screen` or of `occ_screen` or of `vir_screen` on one device may be relied on, other than what follows from the above.
Results may differ from a plain program's by a relative error of at most 0.0029.
Values may be sent and summed in bfloat16 or wider, within the bound.
A program may use at most 128 MiB of HBM per device.

v0:
```python
import jax
import jax.numpy as jnp
from jax import lax
from jax.sharding import PartitionSpec as P


def with_halo(block, sides, width):
    for axis, dim in sides:
        count = lax.axis_size(axis)
        forward = [(i, i + 1) for i in range(count - 1)]
        backward = [(target, source) for source, target in forward]
        low = lax.ppermute(
            lax.slice_in_dim(block, block.shape[dim] - width, None, axis=dim), axis, forward
        )
        high = lax.ppermute(lax.slice_in_dim(block, 0, width, axis=dim), axis, backward)
        block = jnp.concatenate([low, block, high], axis=dim)
    return block


def tile_mask(screen, first, nob, block_size):
    count = screen.shape[0]
    blocks = (
        first
        + jnp.arange(count, dtype=jnp.int32)[:, None]
        + jnp.arange(3, dtype=jnp.int32)[None, :]
        - 1
    )
    live = (screen == 1) & (blocks >= 0) & (blocks < nob)
    return jnp.repeat(jnp.repeat(live, block_size, axis=0), block_size, axis=1)


def per_device(three_centre, b_screen, g_occ, occ_screen, g_vir, vir_screen):
    aux_dev, rows, width = three_centre.shape
    block_size = width // 3
    nbd = rows // block_size
    nob = nbd * lax.axis_size("orb")
    first = lax.axis_index("orb") * nbd
    nothing = jnp.zeros((), jnp.bfloat16)
    every_b = lax.all_to_all(three_centre, "aux", split_axis=1, concat_axis=0, tiled=True)
    b_mask = tile_mask(b_screen, first, nob, block_size)[None]
    kept_b = jnp.where(b_mask, three_centre, nothing)
    kept_o = jnp.where(tile_mask(occ_screen, first, nob, block_size), g_occ, nothing)
    kept_v = jnp.where(tile_mask(vir_screen, first, nob, block_size), g_vir, nothing)
    wide_b = with_halo(kept_b, (("orb", 1),), block_size)
    wide_v = with_halo(kept_v, (("orb", 0),), block_size)
    right = jnp.zeros((aux_dev, nbd, block_size, 5 * block_size), jnp.float32)
    for slot in range(3):
        lower = slot * block_size
        occ_slot = kept_o[:, lower : lower + block_size].reshape(nbd, block_size, block_size)
        near_b = wide_b[:, lower : lower + rows].reshape(aux_dev, nbd, block_size, width)
        term = jnp.einsum("jin,qjnk->qjik", occ_slot, near_b, preferred_element_type=jnp.float32)
        right = right.at[..., lower : lower + width].add(term)
    right_b = right.astype(jnp.bfloat16)
    parts = []
    for slot in range(3):
        lower = slot * block_size
        vir_rows = wide_v[lower : lower + rows].reshape(nbd, block_size, width)
        parts.append(
            jnp.einsum(
                "qjik,jlk->qjil",
                right_b[..., lower : lower + width],
                vir_rows,
                preferred_element_type=jnp.float32,
            )
        )
    w = jnp.concatenate(parts, axis=-1).reshape(aux_dev, rows, width)
    w = jnp.where(b_mask, w, 0.0).astype(jnp.bfloat16)
    every_w = lax.all_to_all(w, "aux", split_axis=1, concat_axis=0, tiled=True)
    partial_value = lax.dot_general(
        every_b, every_w, (((1, 2), (1, 2)), ((), ())), preferred_element_type=jnp.float32
    )
    summed = lax.psum(partial_value, ("orb", "aux"))
    return lax.dynamic_slice_in_dim(summed, lax.axis_index("aux") * aux_dev, aux_dev, 0)


def solution(mesh):
    in_specs = (
        P("aux", "orb", None),
        P("orb", None),
        P("orb", None),
        P("orb", None),
        P("orb", None),
        P("orb", None),
    )
    out_specs = P("aux", None)
    return jax.shard_map(
        per_device, mesh=mesh, in_specs=in_specs, out_specs=out_specs, check_vma=False
    )
```

profile of v0, /device:TPU:0, one launch (start us, length us, event | category | flops | bytes accessed | tf_op | source)
XLA Modules:
  0.0 161.0 jit_solution(2481949846016735281)
XLA Ops:
  0.0 0.8 and_and_fusion.2
  0.8 0.1 copy.36
  0.9 0.1 broadcast_bitcast_fusion.2
  1.1 0.3 copy.37
  1.4 2.5 %broadcast_select_fusion = bf16[8,512,384]{2,1,0:T(8,128)(2,1)S(1)} fusion(bf16[8,512,384]{2,1,0:T(8,128)(2,1)} %param.12, pred[512,384]{1,0:T(8,128)(4,1)S(1)} %copy.37), kind=kLoop, calls=%fused_computation.26 | loop fusion | flops 1572864 | bytes 6488064 | tf_op jit(solution)/shard_map/jit(_where)/select_n | solution.py:41
  3.9 1.4 fusion.43
  5.2 3.2 %collective-permute-start.1 = (bf16[8,128,384]{2,1,0:T(8,128)(2,1)}, bf16[8,128,384]{2,1,0:T(8,128)(2,1)}, u32[]{:S(2)}, u32[]{:S(2)}) collective-permute-start(bf16[8,128,384]{2,1,0:T(8,128)(2,1)} %get-tuple-element.44), channel_id=1, source_target_pairs={{0,4},{4,8},{8,12},{12,16},{16,20},{20,24},{24,28},{1,5},{5,9},{9,... | collective-permute-start | bytes 2359304 | tf_op jit(solution)/shard_map/ppermute | solution.py:12
  8.5 1.3 collective-permute-start.2
  9.8 0.1 copy.38
  9.9 0.1 broadcast_bitcast_fusion.1
  10.0 1.9 %copy.39 = bf16[512,384]{0,1:T(8,128)(2,1)} copy(bf16[512,384]{1,0:T(8,128)(2,1)} %param.16) | data formatting | bytes 786432 | tf_op args[4]
  11.9 1.0 bitcast_select_fusion.2
  12.9 0.7 fusion.44
  13.6 5.0 %collective-permute-start = (bf16[128,384]{0,1:T(8,128)(2,1)}, bf16[128,384]{0,1:T(8,128)(2,1)}, u32[]{:S(2)}, u32[]{:S(2)}) collective-permute-start(bf16[128,384]{0,1:T(8,128)(2,1)} %get-tuple-element.47), channel_id=1, source_target_pairs={{0,4},{4,8},{8,12},{12,16},{16,20},{20,24},{24,28},{1,5},{5,9},{9,... | collective-permute-start | bytes 294920 | tf_op jit(solution)/shard_map/ppermute | solution.py:12
  18.6 1.3 collective-permute-start.3
  19.9 5.4 %copy.57 = bf16[8,512,384]{2,0,1:T(8,128)(2,1)} copy(bf16[8,512,384]{2,1,0:T(8,128)(2,1)} %param.12) | data formatting | bytes 6291456 | tf_op args[0]
  25.4 4.7 %all-to-all-start.1 = ((bf16[8,512,384]{2,0,1:T(8,128)(2,1)}), bf16[8,512,384]{2,0,1:T(8,128)(2,1)}, u32[]{:S(2)}, u32[]{:S(2)}) async-start(bf16[8,512,384]{2,0,1:T(8,128)(2,1)} %copy.57), calls=%async_computation.1 | async-start | bytes 6291456 | tf_op jit(solution)/shard_map/all_to_all | solution.py:39
  30.0 0.1 copy.41
  30.1 0.1 broadcast_bitcast_fusion
  30.2 1.9 %copy.42 = bf16[512,384]{0,1:T(8,128)(2,1)} copy(bf16[512,384]{1,0:T(8,128)(2,1)} %param.14) | data formatting | bytes 786432 | tf_op args[2]
  32.2 1.0 bitcast_select_fusion.1
  33.2 0.8 fusion.45
  34.0 0.9 copy.75
  34.9 1.7 %copy.43 = bf16[512,128]{1,0:T(8,128)(2,1)} copy(bf16[512,128]{0,1:T(8,128)(2,1)} %get-tuple-element.51) | data formatting | bytes 262144 | tf_op jit(solution)/shard_map/slice | solution.py:49
  36.5 1.7 %copy.45 = bf16[512,128]{1,0:T(8,128)(2,1)} copy(bf16[512,128]{0,1:T(8,128)(2,1)} %get-tuple-element.50) | data formatting | bytes 262144 | tf_op jit(solution)/shard_map/slice | solution.py:49
  38.2 1.7 %copy.47 = bf16[512,128]{1,0:T(8,128)(2,1)} copy(bf16[512,128]{0,1:T(8,128)(2,1)} %get-tuple-element.49) | data formatting | bytes 262144 | tf_op jit(solution)/shard_map/slice | solution.py:49
  39.9 1.9 %pad_maximum_fusion.4 = (bf16[512,384]{0,1:T(8,128)(2,1)}, bf16[512,384]{0,1:T(8,128)(2,1)}) fusion(bf16[512,384]{0,1:T(8,128)(2,1)S(1)} %bitcast_select_fusion.2, bf16[128,384]{0,1:T(8,128)(2,1)} %collective-permute-done, bf16[128,384]{0,1:T(8,128)(2,1)} %collective-permute-done.3), kind=kLoop, calls=%fused_computation.35 | loop fusion | flops 1572864 | bytes 1376256 | tf_op jit(solution)/shard_map/concatenate | solution.py:16
  41.8 1.2 copy.40
  43.0 1.9 %copy.52 = bf16[512,384]{1,0:T(8,128)(2,1)} copy(bf16[512,384]{0,1:T(8,128)(2,1)} %get-tuple-element.46) | data formatting | bytes 786432 | tf_op jit(solution)/shard_map/slice | solution.py:57
  44.9 3.1 %pad_maximum_fusion.1 = (bf16[8,512,384]{2,1,0:T(8,128)(2,1)}, bf16[8,512,384]{2,1,0:T(8,128)(2,1)S(1)}) fusion(bf16[8,128,384]{2,1,0:T(8,128)(2,1)} %collective-permute-done.2, bf16[8,512,384]{2,1,0:T(8,128)(2,1)S(1)} %broadcast_select_fusion, bf16[8,128,384]{2,1,0:T(8,128)(2,1)} %collective-permute-done.1), kind=kLoop, calls=%fused_computation.13 | loop fusion | flops 12582912 | bytes 11010048 | tf_op jit(solution)/shard_map/concatenate | solution.py:16
  48.0 1.2 fusion.24
  49.3 1.5 scatter-add.10
  50.8 3.3 %fusion.2 = f32[8,4,128,640]{2,3,0,1:T(8,128)S(1)} fusion(f32[8,4,128,640]{2,3,0,1:T(8,128)S(1)} %scatter-add.10, bf16[4,128,128,1]{2,1,3,0:T(8,128)(2,1)S(1)} %bitcast.109, bf16[8,4,128,384]{3,2,1,0:T(8,128)(2,1)S(1)} %bitcast.103), kind=kOutput, calls=%fused_computation.6 | convolution fusion | flops 404226048 | bytes 15859712 | tf_op jit(solution)/shard_map/jin,qjnk->qjik/dot_general | solution.py:51
  54.1 3.3 %fusion = f32[8,4,128,640]{2,3,0,1:T(8,128)S(1)} fusion(f32[8,4,128,640]{2,3,0,1:T(8,128)S(1)} %fusion.2, bf16[4,128,128,1]{2,1,3,0:T(8,128)(2,1)S(1)} %bitcast.108, bf16[8,4,128,384]{3,2,1,0:T(8,128)(2,1)S(1)} %bitcast.105), kind=kOutput, calls=%fused_computation.1 | convolution fusion | flops 404226048 | bytes 15859712 | tf_op jit(solution)/shard_map/jin,qjnk->qjik/dot_general | solution.py:51
  57.3 3.1 %convert_element_type.6 = bf16[8,4,128,640]{2,3,0,1:T(8,128)(2,1)} convert(f32[8,4,128,640]{2,3,0,1:T(8,128)S(1)} %fusion) | non-fusion elementwise | flops 2621440 | bytes 15728640 | tf_op jit(solution)/shard_map/convert_element_type | solution.py:53
  60.5 2.8 %fusion.27 = bf16[8,4,128,128]{2,3,0,1:T(8,128)(2,1)S(1)} fusion(bf16[4,128,384,1]{2,1,3,0:T(8,128)(2,1)S(1)} %bitcast.112, bf16[8,4,128,640]{2,3,0,1:T(8,128)(2,1)} %convert_element_type.6), kind=kOutput, calls=%fused_computation.28 | convolution fusion | flops 402653184 | bytes 4587520 | tf_op jit(solution)/shard_map/qjik,jlk->qjil/dot_general | solution.py:59
  63.2 2.7 %fusion.33 = bf16[8,4,128,128]{2,3,0,1:T(8,128)(2,1)S(1)} fusion(bf16[4,128,384,1]{2,1,3,0:T(8,128)(2,1)S(1)} %bitcast.113, bf16[8,4,128,640]{2,3,0,1:T(8,128)(2,1)} %convert_element_type.6), kind=kOutput, calls=%fused_computation.30 | convolution fusion | flops 402653184 | bytes 4587520 | tf_op jit(solution)/shard_map/qjik,jlk->qjil/dot_general | solution.py:59
  65.9 0.7 fusion.30
  66.7 0.3 pad_maximum_fusion
  67.0 2.8 %copy.54 = bf16[8,4,128,384]{3,2,1,0:T(8,128)(2,1)} copy(bf16[8,4,128,384]{2,3,0,1:T(8,128)(2,1)S(1)} %pad_maximum_fusion) | data formatting | bytes 6291456 | tf_op jit(solution)/shard_map/concatenate | solution.py:66
  69.8 2.5 %fusion.1 = bf16[8,512,384]{2,1,0:T(8,128)(2,1)S(1)} fusion(bf16[8,4,128,384]{3,2,1,0:T(8,128)(2,1)} %copy.54, pred[512,384]{1,0:T(8,128)(4,1)S(1)} %copy-done.3), kind=kLoop, calls=%fused_computation.4 | loop fusion | flops 1572864 | bytes 6488064 | tf_op jit(solution)/shard_map/convert_element_type | solution.py:67
  72.4 3.5 %copy.55 = bf16[8,512,384]{2,0,1:T(8,128)(2,1)} copy(bf16[8,512,384]{2,1,0:T(8,128)(2,1)S(1)} %fusion.1) | data formatting | bytes 6291456 | tf_op jit(solution)/shard_map/convert_element_type | solution.py:67
  75.9 4.2 %all-to-all-start = ((bf16[8,512,384]{2,0,1:T(8,128)(2,1)}), bf16[8,512,384]{2,0,1:T(8,128)(2,1)S(1)}, u32[]{:S(2)}, u32[]{:S(2)}) async-start(bf16[8,512,384]{2,0,1:T(8,128)(2,1)} %copy.55), calls=%async_computation | async-start | bytes 6291456 | tf_op jit(solution)/shard_map/all_to_all | solution.py:68
  80.0 37.2 %all-to-all-done = bf16[8,512,384]{2,0,1:T(8,128)(2,1)S(1)} async-done(((bf16[8,512,384]{2,0,1:T(8,128)(2,1)}), bf16[8,512,384]{2,0,1:T(8,128)(2,1)S(1)}, u32[]{:S(2)}, u32[]{:S(2)}) %all-to-all-start) | async-done | bytes 3145760 | tf_op jit(solution)/shard_map/all_to_all | solution.py:68
  117.3 2.8 %fusion.36 = f32[32,32]{0,1:T(8,128)S(1)} fusion(bf16[8,4,128,384]{3,0,2,1:T(8,128)(2,1)} %bitcast.34, bf16[8,4,128,384]{3,0,2,1:T(8,128)(2,1)S(1)} %bitcast.106), kind=kOutput, calls=%fused_computation.31 | convolution fusion | flops 100663296 | bytes 6295552 | tf_op jit(solution)/shard_map/dot_general | solution.py:69
  120.1 40.1 %psum.7 = f32[32,32]{0,1:T(8,128)S(1)} all-reduce(f32[32,32]{0,1:T(8,128)S(1)} %fusion.36), channel_id=1, replica_groups=mesh['orb'=8,'aux'=4] {'orb','aux'}, use_global_device_ids=true, to_apply=%region_0.1 | all-reduce | flops 1024 | bytes 8192 | tf_op jit(solution)/shard_map/psum | solution.py:72
  160.2 0.1 constant_dynamic-slice_fusion
  160.3 0.7 copy.59
  (28 shorter events, 0.1 us)
Async XLA Ops:
  1.4 2.5 %copy-start.2 = (pred[512,384]{1,0:T(8,128)(4,1)}, pred[512,384]{1,0:T(8,128)(4,1)S(1)}, u32[]{:S(2)}) copy-start(pred[512,384]{1,0:T(8,128)(4,1)S(1)} %copy.37) | copy-start | bytes 589828
  5.2 39.7 %collective-permute-start.1 = (bf16[8,128,384]{2,1,0:T(8,128)(2,1)}, bf16[8,128,384]{2,1,0:T(8,128)(2,1)}, u32[]{:S(2)}, u32[]{:S(2)}) collective-permute-start(bf16[8,128,384]{2,1,0:T(8,128)(2,1)} %get-tuple-element.44), channel_id=1, source_target_pairs={{0,4},{4,8},{8,12},{12,16},{16,20},{20,24},{24,28},{1,5},{5,9},{9,... | collective-permute-start | bytes 2359304 | tf_op jit(solution)/shard_map/ppermute | solution.py:12
  8.5 36.4 %collective-permute-start.2 = (bf16[8,128,384]{2,1,0:T(8,128)(2,1)}, bf16[8,128,384]{2,1,0:T(8,128)(2,1)}, u32[]{:S(2)}, u32[]{:S(2)}) collective-permute-start(bf16[8,128,384]{2,1,0:T(8,128)(2,1)} %get-tuple-element.43), channel_id=1, source_target_pairs={{4,0},{8,4},{12,8},{16,12},{20,16},{24,20},{28,24},{5,1},{9,5},{13... | collective-permute-start | bytes 2359304 | tf_op jit(solution)/shard_map/ppermute | solution.py:15
  13.6 26.2 %collective-permute-start = (bf16[128,384]{0,1:T(8,128)(2,1)}, bf16[128,384]{0,1:T(8,128)(2,1)}, u32[]{:S(2)}, u32[]{:S(2)}) collective-permute-start(bf16[128,384]{0,1:T(8,128)(2,1)} %get-tuple-element.47), channel_id=1, source_target_pairs={{0,4},{4,8},{8,12},{12,16},{16,20},{20,24},{24,28},{1,5},{5,9},{9,... | collective-permute-start | bytes 294920 | tf_op jit(solution)/shard_map/ppermute | solution.py:12
  18.6 21.2 %collective-permute-start.3 = (bf16[128,384]{0,1:T(8,128)(2,1)}, bf16[128,384]{0,1:T(8,128)(2,1)}, u32[]{:S(2)}, u32[]{:S(2)}) collective-permute-start(bf16[128,384]{0,1:T(8,128)(2,1)} %get-tuple-element.48), channel_id=1, source_target_pairs={{4,0},{8,4},{12,8},{16,12},{20,16},{24,20},{28,24},{5,1},{9,5},{13... | collective-permute-start | bytes 294920 | tf_op jit(solution)/shard_map/ppermute | solution.py:15
  25.4 50.5 %all-to-all-start.1 = ((bf16[8,512,384]{2,0,1:T(8,128)(2,1)}), bf16[8,512,384]{2,0,1:T(8,128)(2,1)}, u32[]{:S(2)}, u32[]{:S(2)}) async-start(bf16[8,512,384]{2,0,1:T(8,128)(2,1)} %copy.57), calls=%async_computation.1 | async-start | bytes 6291456 | tf_op jit(solution)/shard_map/all_to_all | solution.py:39
  44.9 3.1 %copy-start.6 = (bf16[512,128]{1,0:T(8,128)(2,1)S(1)}, bf16[512,128]{1,0:T(8,128)(2,1)}, u32[]{:S(2)}) copy-start(bf16[512,128]{1,0:T(8,128)(2,1)} %copy.43) | copy-start | bytes 393220
  49.3 1.5 copy-start.5
  50.8 3.3 %copy-start = (bf16[8,512,384]{2,1,0:T(8,128)(2,1)S(1)}, bf16[8,512,384]{2,1,0:T(8,128)(2,1)}, u32[]{:S(2)}) copy-start(bf16[8,512,384]{2,1,0:T(8,128)(2,1)} %get-tuple-element.41) | copy-start | bytes 9437188
  50.8 3.3 %copy-start.4 = (bf16[512,128]{1,0:T(8,128)(2,1)S(1)}, bf16[512,128]{1,0:T(8,128)(2,1)}, u32[]{:S(2)}) copy-start(bf16[512,128]{1,0:T(8,128)(2,1)} %copy.47) | copy-start | bytes 393220
  60.5 2.8 %copy-start.8 = (bf16[512,384]{1,0:T(8,128)(2,1)S(1)}, bf16[512,384]{1,0:T(8,128)(2,1)}, u32[]{:S(2)}) copy-start(bf16[512,384]{1,0:T(8,128)(2,1)} %copy.52) | copy-start | bytes 1179652
  60.5 5.5 %copy-start.1 = (bf16[8,4,128,640]{2,3,0,1:T(8,128)(2,1)S(1)}, bf16[8,4,128,640]{2,3,0,1:T(8,128)(2,1)}, u32[]{:S(2)}) copy-start(bf16[8,4,128,640]{2,3,0,1:T(8,128)(2,1)} %convert_element_type.6) | copy-start | bytes 15728644
  63.2 2.7 %copy-start.7 = (bf16[512,384]{1,0:T(8,128)(2,1)S(1)}, bf16[512,384]{1,0:T(8,128)(2,1)}, u32[]{:S(2)}) copy-start(bf16[512,384]{1,0:T(8,128)(2,1)} %copy.75) | copy-start | bytes 1179652
  67.0 2.8 %copy-start.3 = (pred[512,384]{1,0:T(8,128)(4,1)S(1)}, pred[512,384]{1,0:T(8,128)(4,1)}, u32[]{:S(2)}) copy-start(pred[512,384]{1,0:T(8,128)(4,1)} %copy-done.2) | copy-start | bytes 589828
  75.9 41.4 %all-to-all-start = ((bf16[8,512,384]{2,0,1:T(8,128)(2,1)}), bf16[8,512,384]{2,0,1:T(8,128)(2,1)S(1)}, u32[]{:S(2)}, u32[]{:S(2)}) async-start(bf16[8,512,384]{2,0,1:T(8,128)(2,1)} %copy.55), calls=%async_computation | async-start | bytes 6291456 | tf_op jit(solution)/shard_map/all_to_all | solution.py:68
where the time goes:
time: 162 us; the launch traced here: 161 us
  blocking collectives  40.1 us (25%)
  waiting for transfers between devices  37.3 us (23%)
  local copies, waits for them, and re-layouts  30.7 us (19%)
  starting transfers between devices  19.6 us (12%)
  matrix products  16.7 us (10%)
  other arithmetic  16.3 us (10%)
    psum x1, blocking collectives, per_device(): summed = lax.psum(partial_value, ('orb', 'aux'))  40.1 us
    all_to_all x1, waiting for transfers between devices, per_device(): every_w = lax.all_to_all(w, 'aux', split_axis=1, concat_axis=0, tiled=True)  37.2 us
    unnamed x27, local copies, waits for them, and re-layouts  9.6 us
    ppermute x2, starting transfers between devices, with_halo(): lax.ppermute(lax.slice_in_dim(block, block.shape[dim] - width, None, axis...  8.24 us
    dot_general x3, matrix products, per_device(): jnp.einsum('jin,qjnk->qjik', occ_slot, near_b, preferred_element_type=jnp...  7.75 us
    dot_general x3, matrix products, per_device(): jnp.einsum('qjik,jlk->qjil', right_b[..., lower:lower + width], vir_rows,...  6.14 us
    slice x4, local copies, waits for them, and re-layouts, per_device(): kept_o[:, lower:lower + block_size].reshape(nbd, block_size, block_size)  5.76 us
    concatenate x2, other arithmetic, with_halo(): block = jnp.concatenate([low, block, high], axis=dim)  5.03 us
  transfers between devices with their start and end apart: 6, of which 1 were waited for; matrix products, arithmetic and copies ran while one was open for 34% of the time, Pallas kernels for 0%

commit v1 on v0

--- a/solution.py
+++ b/solution.py
@@ -69,7 +69,8 @@
     partial_value = lax.dot_general(
         every_b, every_w, (((1, 2), (1, 2)), ((), ())), preferred_element_type=jnp.float32
     )
-    summed = lax.psum(partial_value, ("orb", "aux"))
+    pieces = lax.all_gather(partial_value, ("orb", "aux"), axis=0, tiled=False)
+    summed = pieces.sum(axis=0)
     return lax.dynamic_slice_in_dim(summed, lax.axis_index("aux") * aux_dev, aux_dev, 0)
 
 

time: 162 us -> 190 us (1.17)
  blocking collectives: 40.1 us -> 68.7 us
    all_gather x0 -> x1, blocking collectives: none -> 68.7 us  [per_device(): pieces = lax.all_gather(partial_value, ('orb', 'aux'), axis=0, tiled=False)]
    psum x1 -> x0, blocking collectives: 40.1 us -> none  [per_device(): summed = lax.psum(partial_value, ('orb', 'aux'))]
  transfers between devices with their start and end apart: 6 -> 6, of which waited for: 1 -> 1; matrix products, arithmetic and copies ran while one was open for 34% -> 29% of each run, Pallas kernels for 0% -> 0%
where the time goes in v1:
time: 190 us
  blocking collectives  68.7 us (36%)
  waiting for transfers between devices  37.3 us (20%)
  local copies, waits for them, and re-layouts  30.7 us (16%)
  starting transfers between devices  19.6 us (10%)
  matrix products  16.7 us (9%)
  other arithmetic  16.4 us (9%)
    all_gather x1, blocking collectives, per_device(): pieces = lax.all_gather(partial_value, ('orb', 'aux'), axis=0, tiled=False)  68.7 us
    all_to_all x1, waiting for transfers between devices, per_device(): every_w = lax.all_to_all(w, 'aux', split_axis=1, concat_axis=0, tiled=True)  37.2 us
    unnamed x27, local copies, waits for them, and re-layouts  9.6 us
    ppermute x2, starting transfers between devices, with_halo(): lax.ppermute(lax.slice_in_dim(block, block.shape[dim] - width, None, axis...  8.24 us
    dot_general x3, matrix products, per_device(): jnp.einsum('jin,qjnk->qjik', occ_slot, near_b, preferred_element_type=jnp...  7.75 us
    dot_general x3, matrix products, per_device(): jnp.einsum('qjik,jlk->qjil', right_b[..., lower:lower + width], vir_rows,...  6.14 us
    slice x4, local copies, waits for them, and re-layouts, per_device(): kept_o[:, lower:lower + block_size].reshape(nbd, block_size, block_size)  5.76 us
    concatenate x2, other arithmetic, with_halo(): block = jnp.concatenate([low, block, high], axis=dim)  5.03 us
  transfers between devices with their start and end apart: 6, of which 1 were waited for; matrix products, arithmetic and copies ran while one was open for 29% of the time, Pallas kernels for 0%

profile of v1, /device:TPU:0, one launch (start us, length us, event | category | flops | bytes accessed | tf_op | source)
XLA Modules:
  0.0 189.5 jit_solution(12322322102036500226)
XLA Ops:
  0.0 0.8 and_and_fusion.2
  0.8 0.1 copy.34
  0.9 0.1 broadcast_bitcast_fusion.2
  1.1 0.3 copy.35
  1.4 2.5 %broadcast_select_fusion = bf16[8,512,384]{2,1,0:T(8,128)(2,1)S(1)} fusion(bf16[8,512,384]{2,1,0:T(8,128)(2,1)} %param.12, pred[512,384]{1,0:T(8,128)(4,1)S(1)} %copy.35), kind=kLoop, calls=%fused_computation.26 | loop fusion | flops 1572864 | bytes 6488064 | tf_op jit(solution)/shard_map/jit(_where)/select_n | solution.py:41
  3.9 1.4 fusion.43
  5.2 3.2 %collective-permute-start.1 = (bf16[8,128,384]{2,1,0:T(8,128)(2,1)}, bf16[8,128,384]{2,1,0:T(8,128)(2,1)}, u32[]{:S(2)}, u32[]{:S(2)}) collective-permute-start(bf16[8,128,384]{2,1,0:T(8,128)(2,1)} %get-tuple-element.44), channel_id=1, source_target_pairs={{0,4},{4,8},{8,12},{12,16},{16,20},{20,24},{24,28},{1,5},{5,9},{9,... | collective-permute-start | bytes 2359304 | tf_op jit(solution)/shard_map/ppermute | solution.py:12
  8.5 1.3 collective-permute-start.2
  9.8 0.1 copy.36
  9.9 0.1 broadcast_bitcast_fusion.1
  10.0 1.9 %copy.37 = bf16[512,384]{0,1:T(8,128)(2,1)} copy(bf16[512,384]{1,0:T(8,128)(2,1)} %param.16) | data formatting | bytes 786432 | tf_op args[4]
  11.9 1.0 bitcast_select_fusion.2
  12.9 0.7 fusion.44
  13.6 5.0 %collective-permute-start = (bf16[128,384]{0,1:T(8,128)(2,1)}, bf16[128,384]{0,1:T(8,128)(2,1)}, u32[]{:S(2)}, u32[]{:S(2)}) collective-permute-start(bf16[128,384]{0,1:T(8,128)(2,1)} %get-tuple-element.47), channel_id=1, source_target_pairs={{0,4},{4,8},{8,12},{12,16},{16,20},{20,24},{24,28},{1,5},{5,9},{9,... | collective-permute-start | bytes 294920 | tf_op jit(solution)/shard_map/ppermute | solution.py:12
  18.6 1.3 collective-permute-start.3
  19.9 5.4 %copy.55 = bf16[8,512,384]{2,0,1:T(8,128)(2,1)} copy(bf16[8,512,384]{2,1,0:T(8,128)(2,1)} %param.12) | data formatting | bytes 6291456 | tf_op args[0]
  25.4 4.7 %all-to-all-start.1 = ((bf16[8,512,384]{2,0,1:T(8,128)(2,1)}), bf16[8,512,384]{2,0,1:T(8,128)(2,1)}, u32[]{:S(2)}, u32[]{:S(2)}) async-start(bf16[8,512,384]{2,0,1:T(8,128)(2,1)} %copy.55), calls=%async_computation.1 | async-start | bytes 6291456 | tf_op jit(solution)/shard_map/all_to_all | solution.py:39
  30.0 0.1 copy.39
  30.1 0.1 broadcast_bitcast_fusion
  30.2 1.9 %copy.40 = bf16[512,384]{0,1:T(8,128)(2,1)} copy(bf16[512,384]{1,0:T(8,128)(2,1)} %param.14) | data formatting | bytes 786432 | tf_op args[2]
  32.2 1.0 bitcast_select_fusion.1
  33.2 0.8 fusion.45
  34.0 0.9 copy.75
  34.9 1.7 copy.41
  36.5 1.7 copy.43
  38.2 1.7 copy.45
  39.9 1.9 %pad_maximum_fusion.4 = (bf16[512,384]{0,1:T(8,128)(2,1)}, bf16[512,384]{0,1:T(8,128)(2,1)}) fusion(bf16[512,384]{0,1:T(8,128)(2,1)S(1)} %bitcast_select_fusion.2, bf16[128,384]{0,1:T(8,128)(2,1)} %collective-permute-done, bf16[128,384]{0,1:T(8,128)(2,1)} %collective-permute-done.3), kind=kLoop, calls=%fused_computation.35 | loop fusion | flops 1572864 | bytes 1376256 | tf_op jit(solution)/shard_map/concatenate | solution.py:16
  41.8 1.2 copy.38
  43.0 1.9 %copy.50 = bf16[512,384]{1,0:T(8,128)(2,1)} copy(bf16[512,384]{0,1:T(8,128)(2,1)} %get-tuple-element.46) | data formatting | bytes 786432 | tf_op jit(solution)/shard_map/slice | solution.py:57
  44.9 3.1 %pad_maximum_fusion.1 = (bf16[8,512,384]{2,1,0:T(8,128)(2,1)}, bf16[8,512,384]{2,1,0:T(8,128)(2,1)S(1)}) fusion(bf16[8,128,384]{2,1,0:T(8,128)(2,1)} %collective-permute-done.2, bf16[8,512,384]{2,1,0:T(8,128)(2,1)S(1)} %broadcast_select_fusion, bf16[8,128,384]{2,1,0:T(8,128)(2,1)} %collective-permute-done.1), kind=kLoop, calls=%fused_computation.13 | loop fusion | flops 12582912 | bytes 11010048 | tf_op jit(solution)/shard_map/concatenate | solution.py:16
  48.0 1.2 fusion.24
  49.3 1.5 scatter-add.10
  50.8 3.3 %fusion.2 = f32[8,4,128,640]{2,3,0,1:T(8,128)S(1)} fusion(f32[8,4,128,640]{2,3,0,1:T(8,128)S(1)} %scatter-add.10, bf16[4,128,128,1]{2,1,3,0:T(8,128)(2,1)S(1)} %bitcast.111, bf16[8,4,128,384]{3,2,1,0:T(8,128)(2,1)S(1)} %bitcast.104), kind=kOutput, calls=%fused_computation.6 | convolution fusion | flops 404226048 | bytes 15859712 | tf_op jit(solution)/shard_map/jin,qjnk->qjik/dot_general | solution.py:51
  54.1 3.3 %fusion = f32[8,4,128,640]{2,3,0,1:T(8,128)S(1)} fusion(f32[8,4,128,640]{2,3,0,1:T(8,128)S(1)} %fusion.2, bf16[4,128,128,1]{2,1,3,0:T(8,128)(2,1)S(1)} %bitcast.110, bf16[8,4,128,384]{3,2,1,0:T(8,128)(2,1)S(1)} %bitcast.106), kind=kOutput, calls=%fused_computation.1 | convolution fusion | flops 404226048 | bytes 15859712 | tf_op jit(solution)/shard_map/jin,qjnk->qjik/dot_general | solution.py:51
  57.3 3.1 %convert_element_type.6 = bf16[8,4,128,640]{2,3,0,1:T(8,128)(2,1)} convert(f32[8,4,128,640]{2,3,0,1:T(8,128)S(1)} %fusion) | non-fusion elementwise | flops 2621440 | bytes 15728640 | tf_op jit(solution)/shard_map/convert_element_type | solution.py:53
  60.5 2.8 %fusion.27 = bf16[8,4,128,128]{2,3,0,1:T(8,128)(2,1)S(1)} fusion(bf16[4,128,384,1]{2,1,3,0:T(8,128)(2,1)S(1)} %bitcast.114, bf16[8,4,128,640]{2,3,0,1:T(8,128)(2,1)} %convert_element_type.6), kind=kOutput, calls=%fused_computation.28 | convolution fusion | flops 402653184 | bytes 4587520 | tf_op jit(solution)/shard_map/qjik,jlk->qjil/dot_general | solution.py:59
  63.2 2.7 %fusion.33 = bf16[8,4,128,128]{2,3,0,1:T(8,128)(2,1)S(1)} fusion(bf16[4,128,384,1]{2,1,3,0:T(8,128)(2,1)S(1)} %bitcast.115, bf16[8,4,128,640]{2,3,0,1:T(8,128)(2,1)} %convert_element_type.6), kind=kOutput, calls=%fused_computation.30 | convolution fusion | flops 402653184 | bytes 4587520 | tf_op jit(solution)/shard_map/qjik,jlk->qjil/dot_general | solution.py:59
  65.9 0.7 fusion.30
  66.7 0.3 pad_maximum_fusion
  67.0 2.8 %copy.52 = bf16[8,4,128,384]{3,2,1,0:T(8,128)(2,1)} copy(bf16[8,4,128,384]{2,3,0,1:T(8,128)(2,1)S(1)} %pad_maximum_fusion) | data formatting | bytes 6291456 | tf_op jit(solution)/shard_map/concatenate | solution.py:66
  69.8 2.5 %fusion.1 = bf16[8,512,384]{2,1,0:T(8,128)(2,1)S(1)} fusion(bf16[8,4,128,384]{3,2,1,0:T(8,128)(2,1)} %copy.52, pred[512,384]{1,0:T(8,128)(4,1)S(1)} %copy-done.3), kind=kLoop, calls=%fused_computation.4 | loop fusion | flops 1572864 | bytes 6488064 | tf_op jit(solution)/shard_map/convert_element_type | solution.py:67
  72.4 3.5 %copy.53 = bf16[8,512,384]{2,0,1:T(8,128)(2,1)} copy(bf16[8,512,384]{2,1,0:T(8,128)(2,1)S(1)} %fusion.1) | data formatting | bytes 6291456 | tf_op jit(solution)/shard_map/convert_element_type | solution.py:67
  75.9 4.2 %all-to-all-start = ((bf16[8,512,384]{2,0,1:T(8,128)(2,1)}), bf16[8,512,384]{2,0,1:T(8,128)(2,1)S(1)}, u32[]{:S(2)}, u32[]{:S(2)}) async-start(bf16[8,512,384]{2,0,1:T(8,128)(2,1)} %copy.53), calls=%async_computation | async-start | bytes 6291456 | tf_op jit(solution)/shard_map/all_to_all | solution.py:68
  80.0 37.2 %all-to-all-done = bf16[8,512,384]{2,0,1:T(8,128)(2,1)S(1)} async-done(((bf16[8,512,384]{2,0,1:T(8,128)(2,1)}), bf16[8,512,384]{2,0,1:T(8,128)(2,1)S(1)}, u32[]{:S(2)}, u32[]{:S(2)}) %all-to-all-start) | async-done | bytes 3145760 | tf_op jit(solution)/shard_map/all_to_all | solution.py:68
  117.3 2.8 %fusion.36 = f32[32,32]{0,1:T(8,128)S(1)} fusion(bf16[8,4,128,384]{3,0,2,1:T(8,128)(2,1)} %bitcast.34, bf16[8,4,128,384]{3,0,2,1:T(8,128)(2,1)S(1)} %bitcast.107), kind=kOutput, calls=%fused_computation.31 | convolution fusion | flops 100663296 | bytes 6295552 | tf_op jit(solution)/shard_map/dot_general | solution.py:69
  120.1 0.1 copy.57
  120.2 68.7 %all-gather = f32[1024,32]{1,0:T(8,128)S(1)} all-gather(f32[32,32]{1,0:T(8,128)S(1)} %copy.57), channel_id=2, replica_groups=mesh['orb'=8,'aux'=4] {'orb','aux'}, dimensions={0}, use_global_device_ids=true | all-gather | bytes 135168 | tf_op jit(solution)/shard_map/all_gather | solution.py:72
  188.9 0.6 constant_dynamic-slice_fusion
  (29 shorter events, 0.2 us)
Async XLA Ops:
  1.4 2.5 %copy-start.2 = (pred[512,384]{1,0:T(8,128)(4,1)}, pred[512,384]{1,0:T(8,128)(4,1)S(1)}, u32[]{:S(2)}) copy-start(pred[512,384]{1,0:T(8,128)(4,1)S(1)} %copy.35) | copy-start | bytes 589828
  5.2 39.7 %collective-permute-start.1 = (bf16[8,128,384]{2,1,0:T(8,128)(2,1)}, bf16[8,128,384]{2,1,0:T(8,128)(2,1)}, u32[]{:S(2)}, u32[]{:S(2)}) collective-permute-start(bf16[8,128,384]{2,1,0:T(8,128)(2,1)} %get-tuple-element.44), channel_id=1, source_target_pairs={{0,4},{4,8},{8,12},{12,16},{16,20},{20,24},{24,28},{1,5},{5,9},{9,... | collective-permute-start | bytes 2359304 | tf_op jit(solution)/shard_map/ppermute | solution.py:12
  8.5 36.4 %collective-permute-start.2 = (bf16[8,128,384]{2,1,0:T(8,128)(2,1)}, bf16[8,128,384]{2,1,0:T(8,128)(2,1)}, u32[]{:S(2)}, u32[]{:S(2)}) collective-permute-start(bf16[8,128,384]{2,1,0:T(8,128)(2,1)} %get-tuple-element.43), channel_id=1, source_target_pairs={{4,0},{8,4},{12,8},{16,12},{20,16},{24,20},{28,24},{5,1},{9,5},{13... | collective-permute-start | bytes 2359304 | tf_op jit(solution)/shard_map/ppermute | solution.py:15
  13.6 26.2 %collective-permute-start = (bf16[128,384]{0,1:T(8,128)(2,1)}, bf16[128,384]{0,1:T(8,128)(2,1)}, u32[]{:S(2)}, u32[]{:S(2)}) collective-permute-start(bf16[128,384]{0,1:T(8,128)(2,1)} %get-tuple-element.47), channel_id=1, source_target_pairs={{0,4},{4,8},{8,12},{12,16},{16,20},{20,24},{24,28},{1,5},{5,9},{9,... | collective-permute-start | bytes 294920 | tf_op jit(solution)/shard_map/ppermute | solution.py:12
  18.6 21.2 %collective-permute-start.3 = (bf16[128,384]{0,1:T(8,128)(2,1)}, bf16[128,384]{0,1:T(8,128)(2,1)}, u32[]{:S(2)}, u32[]{:S(2)}) collective-permute-start(bf16[128,384]{0,1:T(8,128)(2,1)} %get-tuple-element.48), channel_id=1, source_target_pairs={{4,0},{8,4},{12,8},{16,12},{20,16},{24,20},{28,24},{5,1},{9,5},{13... | collective-permute-start | bytes 294920 | tf_op jit(solution)/shard_map/ppermute | solution.py:15
  25.4 50.5 %all-to-all-start.1 = ((bf16[8,512,384]{2,0,1:T(8,128)(2,1)}), bf16[8,512,384]{2,0,1:T(8,128)(2,1)}, u32[]{:S(2)}, u32[]{:S(2)}) async-start(bf16[8,512,384]{2,0,1:T(8,128)(2,1)} %copy.55), calls=%async_computation.1 | async-start | bytes 6291456 | tf_op jit(solution)/shard_map/all_to_all | solution.py:39
  44.9 3.1 %copy-start.6 = (bf16[512,128]{1,0:T(8,128)(2,1)S(1)}, bf16[512,128]{1,0:T(8,128)(2,1)}, u32[]{:S(2)}) copy-start(bf16[512,128]{1,0:T(8,128)(2,1)} %copy.41) | copy-start | bytes 393220
  49.3 1.5 copy-start.5
  50.8 3.3 %copy-start = (bf16[8,512,384]{2,1,0:T(8,128)(2,1)S(1)}, bf16[8,512,384]{2,1,0:T(8,128)(2,1)}, u32[]{:S(2)}) copy-start(bf16[8,512,384]{2,1,0:T(8,128)(2,1)} %get-tuple-element.41) | copy-start | bytes 9437188
  50.8 3.3 %copy-start.4 = (bf16[512,128]{1,0:T(8,128)(2,1)S(1)}, bf16[512,128]{1,0:T(8,128)(2,1)}, u32[]{:S(2)}) copy-start(bf16[512,128]{1,0:T(8,128)(2,1)} %copy.45) | copy-start | bytes 393220
  60.5 2.8 %copy-start.8 = (bf16[512,384]{1,0:T(8,128)(2,1)S(1)}, bf16[512,384]{1,0:T(8,128)(2,1)}, u32[]{:S(2)}) copy-start(bf16[512,384]{1,0:T(8,128)(2,1)} %copy.50) | copy-start | bytes 1179652
  60.5 5.5 %copy-start.1 = (bf16[8,4,128,640]{2,3,0,1:T(8,128)(2,1)S(1)}, bf16[8,4,128,640]{2,3,0,1:T(8,128)(2,1)}, u32[]{:S(2)}) copy-start(bf16[8,4,128,640]{2,3,0,1:T(8,128)(2,1)} %convert_element_type.6) | copy-start | bytes 15728644
  63.2 2.7 %copy-start.7 = (bf16[512,384]{1,0:T(8,128)(2,1)S(1)}, bf16[512,384]{1,0:T(8,128)(2,1)}, u32[]{:S(2)}) copy-start(bf16[512,384]{1,0:T(8,128)(2,1)} %copy.75) | copy-start | bytes 1179652
  67.0 2.8 %copy-start.3 = (pred[512,384]{1,0:T(8,128)(4,1)S(1)}, pred[512,384]{1,0:T(8,128)(4,1)}, u32[]{:S(2)}) copy-start(pred[512,384]{1,0:T(8,128)(4,1)} %copy-done.2) | copy-start | bytes 589828
  75.9 41.4 %all-to-all-start = ((bf16[8,512,384]{2,0,1:T(8,128)(2,1)}), bf16[8,512,384]{2,0,1:T(8,128)(2,1)S(1)}, u32[]{:S(2)}, u32[]{:S(2)}) async-start(bf16[8,512,384]{2,0,1:T(8,128)(2,1)} %copy.53), calls=%async_computation | async-start | bytes 6291456 | tf_op jit(solution)/shard_map/all_to_all | solution.py:68
